TPU v7x, 32 devices: a whole 2x2x4 slice. The times are simulated.
32 devices in a mesh: tm: 8 (over z, x), chan: 4 (over y, core).
Axes of the slice: x: 2, y: 2, z: 4, core: 2. Of those that a mesh axis runs over, the one named last changes fastest.
Arguments:
- features: bfloat16 [16384, 1024], P('tm', 'chan'), may hold values from -18 to 18
- rec_start: int32 [16384], P('tm'), may hold values from 0 to 16383, as said below
- rec_end: int32 [16384], P('tm'), may hold values from 1 to 16384, as said below
- w_value: bfloat16 [1024, 1024], P(None, 'chan'), may hold values from -0.1875 to 0.1875
- w_gate: bfloat16 [1024, 1024], P(None, 'chan'), may hold values from -0.1875 to 0.1875
- depth_kernel: bfloat16 [9, 1024], P(None, 'chan'), may hold values from -2 to 2
- norm_gain: bfloat16 [1024], P('chan'), may hold values from 0.099609375 to 1.8984375
- norm_shift: bfloat16 [1024], P('chan'), may hold values from -3 to 3
- w_down: bfloat16 [1024, 1024], P('chan'), may hold values from -0.1875 to 0.1875
Outputs:
- mixed: bfloat16 [16384, 1024], P('tm', 'chan')
Inputs may be any that keep to these rules, and one draw needn't show every extreme that they name: Frames are packed recordings in order: rec_start[t] <= t < rec_end[t], all frames of a recording share both values, and a recording ends where the next starts. Frame 0 is a recording of its own, and so is the last frame. `rec_end`: as for rec_start.
All inputs are finite; a program needn't handle non-finite values.
Results may differ from a plain program's by a relative error of at most 0.012.
Values may be sent and summed in bfloat16 or wider, within the bound.
A program may use at most 64 MiB of HBM per device.

v0:
```python
import jax
import jax.numpy as jnp
from jax import lax
from jax.sharding import PartitionSpec as P


def extended(block, sides, width):
    for axis, dim in sides:
        count = lax.axis_size(axis)
        forward = [(i, i + 1) for i in range(count - 1)]
        backward = [(target, source) for source, target in forward]
        low = lax.ppermute(
            lax.slice_in_dim(block, block.shape[dim] - width, None, axis=dim), axis, forward
        )
        high = lax.ppermute(lax.slice_in_dim(block, 0, width, axis=dim), axis, backward)
        block = jnp.concatenate([low, block, high], axis=dim)
    return block


def depthwise(padded, starts, ends, first, kernel):
    count = starts.shape[0]
    half = kernel.shape[0] // 2
    frames = first + jnp.arange(count, dtype=jnp.int32)
    conv = jnp.zeros((count, padded.shape[1]), jnp.float32)
    for tap in range(kernel.shape[0]):
        source = frames + (tap - half)
        usable = (source >= starts) & (source < ends)
        term = padded[tap : tap + count].astype(jnp.float32) * kernel[tap].astype(jnp.float32)
        conv = conv + jnp.where(usable[:, None], term, jnp.float32(0.0))
    return conv


def batch_norm(conv, total, single_sum, gain, shift):
    mean = single_sum(jnp.sum(conv, axis=0)) / total
    centred = conv - mean
    var = single_sum(jnp.sum(centred * centred, axis=0)) / total
    normed = centred / jnp.sqrt(var + 1e-05) * gain.astype(jnp.float32) + shift.astype(jnp.float32)
    return (normed * jax.nn.sigmoid(normed)).astype(jnp.bfloat16)


def body(
    features, rec_start, rec_end, w_value, w_gate, depth_kernel, norm_gain, norm_shift, w_down
):
    frame_rows = features.shape[0]
    half = depth_kernel.shape[0] // 2
    n_chan = lax.axis_size("chan")
    total = frame_rows * lax.axis_size("tm")
    piece = lax.all_gather(features, "chan", axis=1, tiled=True)
    value = jnp.dot(piece, w_value, preferred_element_type=jnp.float32)
    gate = jnp.dot(piece, w_gate, preferred_element_type=jnp.float32)
    glu = (value * jax.nn.sigmoid(gate)).astype(jnp.bfloat16)
    padded = extended(glu, (("tm", 0),), half)
    first = lax.axis_index("tm") * frame_rows
    conv = depthwise(padded, rec_start, rec_end, first, depth_kernel)
    swished = batch_norm(conv, total, lambda vector: lax.psum(vector, "tm"), norm_gain, norm_shift)
    down_all = lax.all_gather(w_down, "chan", axis=0, tiled=True)
    out_width = down_all.shape[1] // n_chan
    down_cols = lax.dynamic_slice_in_dim(down_all, lax.axis_index("chan") * out_width, out_width, 1)
    summed = jnp.dot(
        lax.all_gather(swished, "chan", axis=1, tiled=True),
        down_cols,
        preferred_element_type=jnp.float32,
    )
    return summed.astype(jnp.bfloat16)


def solution(mesh):
    in_specs = (
        P("tm", "chan"),
        P("tm"),
        P("tm"),
        P(None, "chan"),
        P(None, "chan"),
        P(None, "chan"),
        P("chan"),
        P("chan"),
        P("chan", None),
    )
    out_specs = P("tm", "chan")
    return jax.shard_map(body, mesh=mesh, in_specs=in_specs, out_specs=out_specs, check_vma=False)
```

profile of v0, /device:TPU:0, one launch (start us, length us, event | category | flops | bytes accessed | tf_op | source)
XLA Modules:
  0.0 149.7 jit_solution(12929976457042439541)
XLA Ops:
  6.5 0.0 copy-start
  6.5 0.0 all-gather.4.cloned.1.call-start
  6.5 0.7 all-gather.4.cloned.1.call-update
  7.3 0.0 all-gather.8.cloned.1.call-start
  7.3 0.7 all-gather.8.cloned.1.call-update
  8.0 0.0 all-gather.6.cloned.1.call-start
  8.1 0.7 fusion.44
  8.8 0.0 copy-start.2
  8.8 37.9 %all-gather.4.cloned.1.call-done = bf16[2048,1024]{1,0:T(8,128)(2,1)} async-done(((bf16[2048,256]{1,0:T(8,128)(2,1)}), bf16[2048,1024]{1,0:T(8,128)(2,1)}) %all-gather.4.cloned.1.call-update) | async-done | bytes 4194320 | tf_op jit(solution)/shard_map/all_gather | solution.py:48
  46.7 0.0 copy-done
  46.7 3.6 %fusion.3 = f32[2048,256]{1,0:T(8,128)S(1)} fusion(bf16[2048,1024]{1,0:T(8,128)(2,1)} %all-gather.4.cloned.1.call-done, bf16[1024,256]{1,0:T(8,128)(2,1)S(1)} %copy-done), kind=kOutput, calls=%fused_computation.6 | convolution fusion | flops 1075314688 | bytes 6815744 | tf_op jit(solution)/shard_map/dot_general | solution.py:50
  50.3 0.0 copy-done.2
  50.3 0.0 copy-done.1
  50.3 0.0 copy-start.3
  50.3 0.0 copy-start.4
  50.3 0.0 copy-start.5
  50.3 1.3 fusion.2
  51.6 1.3 collective-permute-start.1
  52.9 4.5 %collective-permute-start = (bf16[4,256]{1,0:T(4,128)(2,1)S(1)}, bf16[4,256]{1,0:T(4,128)(2,1)S(1)}, u32[]{:S(2)}, u32[]{:S(2)}) collective-permute-start(bf16[4,256]{1,0:T(4,128)(2,1)S(1)} %get-tuple-element.7), channel_id=1, source_target_pairs={{0,4},{4,8},{8,12},{12,16},{16,20},{20,24},{24,28},{1,5},{5,9},{9,... | collective-permute-start | bytes 6152 | tf_op jit(solution)/shard_map/ppermute | solution.py:12
  57.5 0.0 copy-done.3
  57.5 0.0 copy-done.5
  57.5 0.0 collective-permute-done.1
  57.6 1.2 collective-permute-done
  58.8 5.6 %fusion.47 = (f32[256]{0:T(256)S(1)}, f32[2048,256]{1,0:T(8,128)S(1)}) fusion(f32[256]{0:T(256)S(1)} %bitcast.21, bf16[4,256]{1,0:T(4,128)(2,1)S(1)} %collective-permute-done.1, bf16[2048,256]{1,0:T(8,128)(2,1)S(1)} %fusion.2, pred[2048]{0:T(1024)(128)(4,1)S(1)} %get-tuple-element.16, f32[256]{0:T(256)S(1)} %bitcast.22, ...), kind=kLoop, calls=%fused_computation.75 | loop fusion | flops 31457024 | bytes 3178496 | tf_op jit(solution)/shard_map/reduce_sum | solution.py:34
  64.4 22.2 %psum.14 = f32[256]{0:T(256)S(1)} all-reduce(f32[256]{0:T(256)S(1)} %get-tuple-element.5), channel_id=1, replica_groups=mesh['tm'=8,'chan'=4] {'tm'}, use_global_device_ids=true, to_apply=%region_1.2 | all-reduce | flops 256 | bytes 2048 | tf_op jit(solution)/shard_map/psum | solution.py:55
  86.5 0.3 multiply_reduce_fusion
  86.9 17.1 %psum.15 = f32[256]{0:T(256)S(1)} all-reduce(f32[256]{0:T(256)S(1)} %multiply_reduce_fusion), channel_id=1, replica_groups=mesh['tm'=8,'chan'=4] {'tm'}, use_global_device_ids=true, to_apply=%region_3.4 | all-reduce | flops 256 | bytes 2048 | tf_op jit(solution)/shard_map/psum | solution.py:55
  104.0 1.6 %multiply_convert_fusion = bf16[2048,256]{1,0:T(8,128)(2,1)} fusion(f32[2048,256]{1,0:T(8,128)S(1)} %get-tuple-element.6, f32[256]{0:T(256)S(1)} %convert_element_type.71, f32[256]{0:T(256)S(1)} %convert_element_type.70, f32[256]{0:T(256)S(1)} %add_sqrt_fusion, f32[256]{0:T(256)S(1)} %broadcast_multiply_fusion), kind=kLoop, calls=%fused_computation.7 | loop fusion | flops 4718592 | bytes 3149824 | tf_op jit(solution)/shard_map/convert_element_type | solution.py:38
  105.6 0.0 all-gather.6.cloned.1.call-update
  105.7 0.0 all-gather.8.cloned.1.call-done
  105.7 32.9 %all-gather.6.cloned.1.call-done = bf16[2048,1024]{1,0:T(8,128)(2,1)} async-done(((bf16[2048,256]{1,0:T(8,128)(2,1)}), bf16[2048,1024]{1,0:T(8,128)(2,1)}) %all-gather.6.cloned.1.call-update) | async-done | bytes 4194320 | tf_op jit(solution)/shard_map/all_gather | solution.py:60
  138.6 4.5 %convolution_convert_fusion = bf16[2048,256]{1,0:T(8,128)(2,1)} fusion(bf16[2048,1024]{1,0:T(8,128)(2,1)} %all-gather.6.cloned.1.call-done, bf16[1024,1024]{1,0:T(8,128)(2,1)} %all-gather.8.cloned.1.call-done, s32[]{:T(128)S(6)} %select_n.40), kind=kOutput, calls=%fused_computation.5 | convolution fusion | flops 1074266112 | bytes 5767172 | tf_op jit(solution)/shard_map/dot_general | solution.py:59
  (8 shorter events, 0.0 us)
Async XLA Ops:
  6.5 40.1 %copy-start = (bf16[1024,256]{1,0:T(8,128)(2,1)S(1)}, bf16[1024,256]{1,0:T(8,128)(2,1)}, u32[]{:S(2)}) copy-start(bf16[1024,256]{1,0:T(8,128)(2,1)} %param.13) | copy-start | bytes 1572868
  6.5 40.1 %all-gather.4.cloned.1.call-start = ((), (), s32[]{:S(2)}) async-start(), calls=%async_computation | async-start | bytes 5242880 | tf_op jit(solution)/shard_map/all_gather | solution.py:48
  7.3 98.4 %all-gather.8.cloned.1.call-start = ((), (), s32[]{:S(2)}) async-start(), calls=%async_computation.2 | async-start | bytes 2621440 | tf_op jit(solution)/shard_map/all_gather | solution.py:56
  8.0 130.6 %all-gather.6.cloned.1.call-start = ((), (), s32[]{:S(2)}) async-start(), calls=%async_computation.1 | async-start | bytes 5242880 | tf_op jit(solution)/shard_map/all_gather | solution.py:60
  8.8 41.5 %copy-start.2 = (bf16[1024,256]{1,0:T(8,128)(2,1)S(1)}, bf16[1024,256]{1,0:T(8,128)(2,1)}, u32[]{:S(2)}) copy-start(bf16[1024,256]{1,0:T(8,128)(2,1)} %param.12) | copy-start | bytes 1572868
  46.7 3.6 %copy-start.1 = (bf16[2048,1024]{1,0:T(8,128)(2,1)S(1)}, bf16[2048,1024]{1,0:T(8,128)(2,1)}, u32[]{:S(2)}) copy-start(bf16[2048,1024]{1,0:T(8,128)(2,1)} %all-gather.4.cloned.1.call-done) | copy-start | bytes 12582916
  50.3 7.2 %copy-start.3 = (bf16[9,256]{1,0:T(8,128)(2,1)S(1)}, bf16[9,256]{1,0:T(8,128)(2,1)}, u32[]{:S(2)}) copy-start(bf16[9,256]{1,0:T(8,128)(2,1)} %param.14) | copy-start | bytes 13828
  50.3 7.2 %copy-start.4 = (bf16[256]{0:T(256)(128)(2,1)S(1)}, bf16[256]{0:T(256)(128)(2,1)}, u32[]{:S(2)}) copy-start(bf16[256]{0:T(256)(128)(2,1)} %param.16) | copy-start | bytes 1540
  50.3 7.2 %copy-start.5 = (bf16[256]{0:T(256)(128)(2,1)S(1)}, bf16[256]{0:T(256)(128)(2,1)}, u32[]{:S(2)}) copy-start(bf16[256]{0:T(256)(128)(2,1)} %param.15) | copy-start | bytes 1540
  51.6 5.9 %collective-permute-start.1 = (bf16[4,256]{1,0:T(4,128)(2,1)S(1)}, bf16[4,256]{1,0:T(4,128)(2,1)S(1)}, u32[]{:S(2)}, u32[]{:S(2)}) collective-permute-start(bf16[4,256]{1,0:T(4,128)(2,1)S(1)} %get-tuple-element.8), channel_id=1, source_target_pairs={{4,0},{8,4},{12,8},{16,12},{20,16},{24,20},{28,24},{5,1},{9,5},{13... | collective-permute-start | bytes 6152 | tf_op jit(solution)/shard_map/ppermute | solution.py:15
  52.9 5.8 %collective-permute-start = (bf16[4,256]{1,0:T(4,128)(2,1)S(1)}, bf16[4,256]{1,0:T(4,128)(2,1)S(1)}, u32[]{:S(2)}, u32[]{:S(2)}) collective-permute-start(bf16[4,256]{1,0:T(4,128)(2,1)S(1)} %get-tuple-element.7), channel_id=1, source_target_pairs={{0,4},{4,8},{8,12},{12,16},{16,20},{20,24},{24,28},{1,5},{5,9},{9,... | collective-permute-start | bytes 6152 | tf_op jit(solution)/shard_map/ppermute | solution.py:12
Sparse Core Ops, SparseCore 0:
  8.9 37.7 all-gather.3
  48.2 22.5 all-gather.7
  105.8 32.7 all-gather.5
where the time goes:
time: 150 us
  waiting for transfers between devices  73.4 us (49%)
  blocking collectives  39.3 us (26%)
  between operations  13.3 us (9%)
  matrix products  9.39 us (6%)
  other arithmetic  8.34 us (6%)
  starting transfers between devices  5.92 us (4%)
    psum x2, blocking collectives, body(): lax.psum(vector, 'tm')  39.3 us
    all_gather x1, waiting for transfers between devices, body(): piece = lax.all_gather(features, 'chan', axis=1, tiled=True)  37.9 us
    all_gather x1, waiting for transfers between devices, body(): lax.all_gather(swished, 'chan', axis=1, tiled=True)  32.9 us
    reduce_sum x1, other arithmetic, batch_norm(): mean = single_sum(jnp.sum(conv, axis=0)) / total  5.6 us
    ppermute x1, starting transfers between devices, extended(): lax.ppermute(lax.slice_in_dim(block, block.shape[dim] - width, None, axis...  4.55 us
    dot_general x1, matrix products, body(): jnp.dot(lax.all_gather(swished, 'chan', axis=1, tiled=True), down_cols, p...  4.53 us
    dot_general x1, matrix products, body(): gate = jnp.dot(piece, w_gate, preferred_element_type=jnp.float32)  3.6 us
  transfers between devices with their start and end apart: 5, of which 3 were waited for; matrix products, arithmetic and copies ran while one was open for 9% of the time, Pallas kernels for 0%

commit v1 on v0

v1 whole, which is shorter than its diff:
```python
import functools

import jax
import jax.numpy as jnp
from jax import lax
from jax.experimental import pallas as pl
from jax.experimental.pallas import tpu as pltpu
from jax.sharding import PartitionSpec as P

F32, BF16 = jnp.float32, jnp.bfloat16
GROUP = 4
PARTS = 4
STEPS = 8
PAD = 8
BLOCK = 64
LANES = 128


def swish_gate(value, gate):
    return value * (0.5 * jnp.tanh(0.5 * gate) + 0.5)


def kernel(
    n_tm,
    feat, starts, ends, wv, wg, taps, gain, shift, wdown,
    out,
    xg, wo, wd, par, back, fwd, glu, conv, stat, norm, sw, ob,
    loc, wy_s, wy_r, wf_s, wf_r, par_s, par_r, fc_s, fc_r, fy_s, fy_r, ff_s, ff_r,
    ha_s, ha_r, wd_s, wd_r, st_s, st_r, sw_s, sw_r, oy_s, oy_r,
):
    depth, width = wv.shape
    rows = feat.shape[0] // 2
    part, step_rows = rows // PARTS, rows // STEPS
    piece = depth // GROUP
    n_tap = taps.shape[0]
    reach = n_tap // 2
    n_blocks = 2 * n_tm
    total = n_blocks * rows

    t, chan = lax.axis_index("tm"), lax.axis_index("chan")
    y, core = chan // 2, chan % 2
    oy = 1 - y
    me = 2 * t + y
    across = (t, 2 * oy + core)
    beside = (t, 2 * y + 1 - core)
    diag = (t, 2 * oy + 1 - core)
    group, g = t - t % GROUP, t % GROUP

    def at_block(b):
        return (b // 2, 2 * (b % 2) + core)

    def send(src, dst, s, r, to):
        return pltpu.make_async_remote_copy(
            src_ref=src, dst_ref=dst, send_sem=s, recv_sem=r,
            device_id=to, device_id_type=pl.DeviceIdType.MESH,
        )

    def landed(ref, sem):
        pltpu.make_async_copy(ref, ref, sem).wait()

    barrier = pltpu.get_barrier_semaphore()

    def greet(i, c):
        pl.semaphore_signal(
            barrier, inc=1, device_id=at_block((me + i) % n_blocks),
            device_id_type=pl.DeviceIdType.MESH,
        )
        return c

    lax.fori_loop(1, n_blocks, greet, 0)
    for other in (beside, diag):
        pl.semaphore_signal(
            barrier, inc=1, device_id=other, device_id_type=pl.DeviceIdType.MESH
        )
    pl.semaphore_wait(barrier, n_blocks + 1)

    mine = pl.ds(pl.multiple_of(g * piece, piece), piece)
    cross = [
        send(w.at[mine], wo.at[k, mine], wy_s.at[k], wy_r.at[k], across)
        for k, w in enumerate((wv, wg))
    ]
    for copy in cross:
        copy.start()

    def own_rows(i):
        return pl.ds(pl.multiple_of(y * rows + i * part, part), part)

    def other_rows(i):
        return pl.ds(pl.multiple_of(oy * rows + i * part, part), part)

    def part_rows(i):
        return pl.ds(pl.multiple_of(i * part, part), part)

    def order(i):
        return (3 * i) % PARTS

    def feat_beside(i):
        return send(
            feat.at[own_rows(i)], xg.at[chan, part_rows(i)], fc_s.at[i], fc_r.at[i], beside
        )

    def feat_across(i):
        return send(
            feat.at[other_rows(i)], xg.at[chan, part_rows(i)], fy_s.at[i], fy_r.at[i], across
        )

    def feat_forward(i):
        slot = 2 * oy + core
        return send(
            xg.at[slot, part_rows(i)], xg.at[slot, part_rows(i)], ff_s.at[i], ff_r.at[i], beside
        )

    keep = pltpu.make_async_copy(
        feat.at[pl.ds(pl.multiple_of(y * rows, rows), rows)], xg.at[chan], loc.at[0]
    )
    keep.start()
    for i in range(PARTS):
        feat_beside(order(i)).start()

    for q in range(2):
        lanes = slice(q * LANES, (q + 1) * LANES)
        par[2 * y + q] = jnp.zeros(par.shape[1:], F32)
        par[2 * y + q, 0:n_tap, :] = taps[:, lanes].astype(F32)
        par[2 * y + q, n_tap : n_tap + 1, :] = gain[:, lanes].astype(F32)
        par[2 * y + q, n_tap + 1 : n_tap + 2, :] = shift[:, lanes].astype(F32)
    my_par = par.at[pl.ds(2 * y, 2)]
    par_copy = send(my_par, my_par, par_s, par_r, across)
    par_copy.start()

    groups = rows // LANES
    base = t * 2 * rows + y * rows
    span = pl.ds(pl.multiple_of(y * groups, groups), groups)
    frame = (
        base
        + lax.broadcasted_iota(jnp.int32, (groups, LANES), 0) * LANES
        + lax.broadcasted_iota(jnp.int32, (groups, LANES), 1)
    )
    before = jnp.minimum(frame - starts[span, :], reach).astype(F32)
    after = jnp.minimum(ends[span, :] - 1 - frame, reach).astype(F32)
    for r in range(groups):
        tile = slice(r * LANES, (r + 1) * LANES)
        back[tile, :] = jnp.broadcast_to(before[r : r + 1, :], (LANES, LANES)).T
        fwd[tile, :] = jnp.broadcast_to(after[r : r + 1, :], (LANES, LANES)).T

    def share(k, i):
        return send(
            wo.at[k, mine], wo.at[k, mine], wf_s.at[k, i], wf_r.at[k, i],
            (group + (g + i) % GROUP, chan),
        )

    for k in range(2):
        cross[k].wait_recv()
        for i in range(1, GROUP):
            share(k, i).start()
        if k == 0:
            feat_across(order(0)).start()
    for i in range(1, PARTS):
        feat_across(order(i)).start()
    keep.wait()

    def gated(i, half, value_w, gate_w):
        x = jnp.concatenate([xg[j, part_rows(i), :] for j in range(4)], axis=1)
        value = jnp.dot(x, value_w, preferred_element_type=F32)
        gate = jnp.dot(x, gate_w, preferred_element_type=F32)
        both = swish_gate(value, gate).astype(BF16).astype(F32)
        to = pl.ds(pl.multiple_of(PAD + i * part, PAD), part)
        glu[2 * half, to, :] = both[:, :LANES]
        glu[2 * half + 1, to, :] = both[:, LANES:]

    def first_half(n, c):
        i = order(n)
        feat_across(i).wait_recv()
        feat_forward(i).start()
        feat_beside(i).wait_recv()
        feat_forward(i).wait_recv()
        gated(i, y, wv[...], wg[...])
        return c

    lax.fori_loop(0, PARTS, first_half, 0)

    def down_copy(p, h):
        to = (beside, across, diag)[p]
        to_core = to[1] % 2
        cols = pl.ds(pl.multiple_of((2 * h + to_core) * width, width), width)
        held = pl.ds(pl.multiple_of(chan * width, width), width)
        return send(
            wdown.at[:, cols], wd.at[h, held], wd_s.at[p, h], wd_r.at[p, h], to
        )

    for h in range(2):
        cols = pl.ds(pl.multiple_of((2 * h + core) * width, width), width)
        held = pl.ds(pl.multiple_of(chan * width, width), width)
        pltpu.make_async_copy(wdown.at[:, cols], wd.at[h, held], loc.at[1 + h]).start()

    for k in range(2):
        for i in range(1, GROUP):
            share(k, i).wait_recv()

    def second_half(n, c):
        gated(order(n), oy, wo[0], wo[1])
        return c

    lax.fori_loop(0, 2, second_half, 0)
    right = send(
        glu.at[:, pl.ds(rows, PAD)], glu.at[:, pl.ds(0, PAD)], ha_s.at[0], ha_r.at[0],
        at_block((me + 1) % n_blocks),
    )
    left = send(
        glu.at[:, pl.ds(PAD, PAD)], glu.at[:, pl.ds(rows + PAD, PAD)], ha_s.at[1], ha_r.at[1],
        at_block((me + n_blocks - 1) % n_blocks),
    )
    right.start()
    left.start()
    for p in range(3):
        for h in range(2):
            down_copy(p, h).start()
    lax.fori_loop(2, PARTS, second_half, 0)
    par_copy.wait_recv()

    def convolve(q, b):
        at = pl.multiple_of(b * BLOCK, BLOCK)
        room_back, room_fwd = back[pl.ds(at, BLOCK), :], fwd[pl.ds(at, BLOCK), :]
        acc = jnp.zeros((BLOCK, LANES), F32)
        for k in range(n_tap):
            d = k - reach
            term = glu[q, pl.ds(at + (PAD + d), BLOCK), :] * par[q, k : k + 1, :]
            if d < 0:
                term = jnp.where(room_back >= float(-d), term, 0.0)
            elif d > 0:
                term = jnp.where(room_fwd >= float(d), term, 0.0)
            acc = acc + term
        conv[q, pl.ds(at, BLOCK), :] = acc

    n_inner = rows // BLOCK

    def inner(b, c):
        for q in range(4):
            convolve(q, b)
        return c

    lax.fori_loop(1, n_inner - 1, inner, 0)
    right.wait_recv()
    left.wait_recv()
    inner(0, 0)
    inner(n_inner - 1, 0)

    for q in range(4):
        block = conv[q]
        total_q = jnp.sum(block, axis=0, keepdims=True)
        off = block - total_q * (1.0 / rows)
        stat[me, q : q + 1, :] = total_q
        stat[me, 4 + q : 5 + q, :] = jnp.sum(off * off, axis=0, keepdims=True)

    def tell(i, c):
        send(stat.at[me], stat.at[me], st_s, st_r, at_block((me + i) % n_blocks)).start()
        return c

    lax.fori_loop(1, n_blocks, tell, 0)
    landed(stat.at[pl.ds(0, n_blocks - 1)], st_r)
    sums, squares = stat[:, 0:4, :], stat[:, 4:8, :]
    mean = jnp.sum(sums, axis=0) * (1.0 / total)
    drift = sums * (1.0 / rows) - mean[None]
    var = jnp.sum(squares + float(rows) * (drift * drift), axis=0) * (1.0 / total)
    norm[0:4, :] = mean
    norm[4:8, :] = 1.0 / jnp.sqrt(var + 1e-05)

    def step_at(c):
        return pl.ds(pl.multiple_of(c * step_rows, step_rows), step_rows)

    def pass_on(c):
        mid = sw.at[core, :, step_at(c)]
        return send(mid, mid, sw_s.at[c], sw_r.at[c], beside)

    def activate(c):
        for q in range(4):
            scale = norm[4 + q : 5 + q, :] * par[q, n_tap : n_tap + 1, :]
            x = (conv[q, step_at(c), :] - norm[q : q + 1, :]) * scale
            x = x + par[q, n_tap + 1 : n_tap + 2, :]
            lanes = slice((q % 2) * LANES, (q % 2 + 1) * LANES)
            sw[core, q // 2, step_at(c), lanes] = swish_gate(x, x).astype(BF16)
        pass_on(c).start()

    def home_rows(c):
        return pl.ds(pl.multiple_of(y * rows + c * step_rows, step_rows), step_rows)

    def give(c):
        return send(ob.at[step_at(c)], out.at[home_rows(c)], oy_s.at[c], oy_r.at[c], across)

    def project(c):
        pass_on(c).wait_recv()
        x = jnp.concatenate([sw[j % 2, j // 2, step_at(c), :] for j in range(4)], axis=1)
        ob[step_at(c), :] = jnp.dot(x, wd[oy], preferred_element_type=F32).astype(BF16)
        give(c).start()
        out[home_rows(c), :] = jnp.dot(x, wd[y], preferred_element_type=F32).astype(BF16)

    activate(0)
    for h in range(2):
        held = pl.ds(pl.multiple_of(chan * width, width), width)
        pltpu.make_async_copy(
            wdown.at[:, pl.ds(0, width)], wd.at[h, held], loc.at[1 + h]
        ).wait()
        for p in range(3):
            down_copy(p, h).wait_recv()

    def advance(c, carry):
        activate(c + 1)
        project(c)
        return carry

    lax.fori_loop(0, STEPS - 1, advance, 0)
    project(STEPS - 1)

    for copy in cross:
        copy.wait_send()
    par_copy.wait_send()
    right.wait_send()
    left.wait_send()
    for k in range(2):
        for i in range(1, GROUP):
            share(k, i).wait_send()
    for p in range(3):
        for h in range(2):
            down_copy(p, h).wait_send()
    landed(stat.at[pl.ds(0, n_blocks - 1)], st_s)

    def drain(i, c):
        feat_beside(i).wait_send()
        feat_across(i).wait_send()
        feat_forward(i).wait_send()
        return c

    lax.fori_loop(0, PARTS, drain, 0)

    def finish(c, carry):
        pass_on(c).wait_send()
        give(c).wait()
        return carry

    lax.fori_loop(0, STEPS, finish, 0)


def body(
    n_tm,
    features, rec_start, rec_end, w_value, w_gate, depth_kernel, norm_gain, norm_shift, w_down,
):
    frames, width = features.shape
    depth = w_value.shape[0]
    rows = frames // 2
    dma = pltpu.SemaphoreType.DMA
    vmem = pl.BlockSpec(memory_space=pltpu.VMEM)
    n_blocks = 2 * n_tm
    return pl.pallas_call(
        functools.partial(kernel, n_tm),
        out_shape=jax.ShapeDtypeStruct((frames, width), BF16),
        in_specs=[vmem] * 9,
        out_specs=vmem,
        scratch_shapes=[
            pltpu.VMEM((4, rows, width), BF16),
            pltpu.VMEM((2, depth, width), BF16),
            pltpu.VMEM((2, 4 * width, width), BF16),
            pltpu.VMEM((4, 16, LANES), F32),
            pltpu.VMEM((rows, LANES), F32),
            pltpu.VMEM((rows, LANES), F32),
            pltpu.VMEM((4, rows + 2 * PAD, LANES), F32),
            pltpu.VMEM((4, rows, LANES), F32),
            pltpu.VMEM((n_blocks, 8, LANES), F32),
            pltpu.VMEM((8, LANES), F32),
            pltpu.VMEM((2, 2, rows, width), BF16),
            pltpu.VMEM((rows, width), BF16),
            dma((3,)),
            dma((2,)), dma((2,)),
            dma((2, GROUP)), dma((2, GROUP)),
            dma, dma,
            dma((PARTS,)), dma((PARTS,)),
            dma((PARTS,)), dma((PARTS,)),
            dma((PARTS,)), dma((PARTS,)),
            dma((2,)), dma((2,)),
            dma((3, 2)), dma((3, 2)),
            dma, dma,
            dma((STEPS,)), dma((STEPS,)),
            dma((STEPS,)), dma((STEPS,)),
        ],
        compiler_params=pltpu.CompilerParams(
            collective_id=0, has_side_effects=True, vmem_limit_bytes=40 * 1024 * 1024
        ),
    )(
        features,
        rec_start.reshape(-1, LANES),
        rec_end.reshape(-1, LANES),
        w_value,
        w_gate,
        depth_kernel,
        norm_gain.reshape(1, -1),
        norm_shift.reshape(1, -1),
        w_down,
    )


def solution(mesh):
    in_specs = (
        P("tm", "chan"),
        P("tm"),
        P("tm"),
        P(None, "chan"),
        P(None, "chan"),
        P(None, "chan"),
        P("chan"),
        P("chan"),
        P("chan", None),
    )
    return jax.shard_map(
        functools.partial(body, mesh.shape["tm"]),
        mesh=mesh,
        in_specs=in_specs,
        out_specs=P("tm", "chan"),
        check_vma=False,
    )
```

time: 150 us -> 67.3 us (0.45)
  waiting for transfers between devices: 73.4 us -> 0 us
  Pallas kernels: 0 us -> 58.1 us
  blocking collectives: 39.3 us -> 0 us
  between operations: 13.3 us -> 0.02 us
  matrix products: 9.39 us -> 0 us
  local copies, waits for them, and re-layouts: 0.04 us -> 8.72 us
  other arithmetic: 8.34 us -> 0 us
  starting transfers between devices: 5.92 us -> 0 us
    all_gather x3 -> x0, waiting for transfers between devices: 70.8 us -> none  [the longest x1 37.9 us: body(): piece = lax.all_gather(features, 'chan', axis=1, tiled=True)]
    pallas_call x0 -> x1, Pallas kernels: none -> 58.1 us  [body(): pl.pallas_call(functools.partial(kernel, n_tm), out_shape=jax.ShapeDtypeS...]
    psum x2 -> x0, blocking collectives: 39.3 us -> none  [body(): lax.psum(vector, 'tm')]
    dot_general x3 -> x0, matrix products: 9.39 us -> none  [the longest x1 4.53 us: body(): jnp.dot(lax.all_gather(swished, 'chan', axis=1, tiled=True), down_cols, p...]
    unnamed x12 -> x19, local copies, waits for them, and re-layouts: 0.03 us -> 8.71 us
    reduce_sum x2 -> x0, other arithmetic: 5.91 us -> none  [the longest x1 5.6 us: batch_norm(): mean = single_sum(jnp.sum(conv, axis=0)) / total]
    ppermute x2 -> x0, starting transfers between devices: 5.84 us -> none  [the longest x1 4.55 us: extended(): lax.ppermute(lax.slice_in_dim(block, block.shape[dim] - width, None, axis...]
    convert_element_type x3 -> x0, other arithmetic: 1.65 us -> none  [the longest x1 1.65 us: batch_norm(): return (normed * jax.nn.sigmoid(normed)).astype(jnp.bfloat16)]
  transfers between devices with their start and end apart: 5 -> 0, of which waited for: 3 -> 0; matrix products, arithmetic and copies ran while one was open for 9% -> 0% of each run, Pallas kernels for 0% -> 0%
where the time goes in v1:
time: 67.3 us; the launch traced here: 66.9 us
  Pallas kernels  58.1 us (86%)
  local copies, waits for them, and re-layouts  8.72 us (13%)
    pallas_call x1, Pallas kernels, body(): pl.pallas_call(functools.partial(kernel, n_tm), out_shape=jax.ShapeDtypeS...  58.1 us
    unnamed x19, local copies, waits for them, and re-layouts  8.71 us

profile of v1, /device:TPU:0, one launch (start us, length us, event | category | flops | bytes accessed | tf_op | source)
XLA Modules:
  0.0 66.9 jit_solution(8304259310936579791)
XLA Ops:
  0.0 0.0 copy-start.7
  0.0 0.7 copy-done.7
  0.7 0.0 copy-start.8
  0.7 0.6 copy-done.8
  1.3 0.0 copy-start
  1.3 1.2 %copy-done = bf16[2048,256]{1,0:T(8,128)(2,1)S(1)} copy-done((bf16[2048,256]{1,0:T(8,128)(2,1)S(1)}, bf16[2048,256]{1,0:T(8,128)(2,1)}, u32[]{:S(2)}) %copy-start) | copy-done | bytes 1048600
  2.5 0.0 copy-start.1
  2.5 1.0 %copy-done.1 = bf16[1024,256]{1,0:T(8,128)(2,1)S(1)} copy-done((bf16[1024,256]{1,0:T(8,128)(2,1)S(1)}, bf16[1024,256]{1,0:T(8,128)(2,1)}, u32[]{:S(2)}) %copy-start.1) | copy-done | bytes 524312
  3.6 0.0 copy-start.2
  3.6 1.0 %copy-done.2 = bf16[1024,256]{1,0:T(8,128)(2,1)S(1)} copy-done((bf16[1024,256]{1,0:T(8,128)(2,1)S(1)}, bf16[1024,256]{1,0:T(8,128)(2,1)}, u32[]{:S(2)}) %copy-start.2) | copy-done | bytes 524312
  4.6 0.0 copy-start.3
  4.6 1.0 %copy-done.3 = bf16[256,1024]{1,0:T(8,128)(2,1)S(1)} copy-done((bf16[256,1024]{1,0:T(8,128)(2,1)S(1)}, bf16[256,1024]{1,0:T(8,128)(2,1)}, u32[]{:S(2)}) %copy-start.3) | copy-done | bytes 524312
  5.7 0.0 copy-start.4
  5.7 0.7 %copy-done.4 = s32[2048]{0:T(1024)S(1)} copy-done((s32[2048]{0:T(1024)S(1)}, s32[2048]{0:T(1024)}, u32[]{:S(2)}) %copy-start.4) | copy-done | bytes 8216
  6.4 0.0 copy-start.5
  6.4 0.7 %copy-done.5 = s32[2048]{0:T(1024)S(1)} copy-done((s32[2048]{0:T(1024)S(1)}, s32[2048]{0:T(1024)}, u32[]{:S(2)}) %copy-start.5) | copy-done | bytes 8216
  7.1 0.0 copy-start.6
  7.1 0.7 %copy-done.6 = bf16[9,256]{1,0:T(8,128)(2,1)S(1)} copy-done((bf16[9,256]{1,0:T(8,128)(2,1)S(1)}, bf16[9,256]{1,0:T(8,128)(2,1)}, u32[]{:S(2)}) %copy-start.6) | copy-done | bytes 4632
  7.8 58.1 %shard_map.91 = bf16[2048,256]{1,0:T(8,128)(2,1)S(1)} custom-call(bf16[2048,256]{1,0:T(8,128)(2,1)S(1)} %copy-done, s32[16,128]{1,0:T(8,128)S(1)} %bitcast.2, s32[16,128]{1,0:T(8,128)S(1)} %bitcast.3, bf16[1024,256]{1,0:T(8,128)(2,1)S(1)} %copy-done.1, bf16[1024,256]{1,0:T(8,128)(2,1)S(1)} %copy-done.2, bf16[9,256]{1,0:T(8,128)(2,1)S(1)} %copy-done.6, ...), custom_call_target="tpu_custom_call" | custom-call | tf_op jit(solution)/shard_map/pallas_call | solution.py:352
  65.9 1.0 %copy.11 = bf16[2048,256]{1,0:T(8,128)(2,1)} copy(bf16[2048,256]{1,0:T(8,128)(2,1)S(1)} %shard_map.91) | data formatting | bytes 2097152
  (2 shorter events, 0.0 us)
Async XLA Ops:
  0.0 0.7 copy-start.7
  0.7 0.7 copy-start.8
  1.3 1.2 %copy-start = (bf16[2048,256]{1,0:T(8,128)(2,1)S(1)}, bf16[2048,256]{1,0:T(8,128)(2,1)}, u32[]{:S(2)}) copy-start(bf16[2048,256]{1,0:T(8,128)(2,1)} %feat.1) | copy-start | bytes 3145732
  2.5 1.0 %copy-start.1 = (bf16[1024,256]{1,0:T(8,128)(2,1)S(1)}, bf16[1024,256]{1,0:T(8,128)(2,1)}, u32[]{:S(2)}) copy-start(bf16[1024,256]{1,0:T(8,128)(2,1)} %wv.1) | copy-start | bytes 1572868
  3.6 1.0 %copy-start.2 = (bf16[1024,256]{1,0:T(8,128)(2,1)S(1)}, bf16[1024,256]{1,0:T(8,128)(2,1)}, u32[]{:S(2)}) copy-start(bf16[1024,256]{1,0:T(8,128)(2,1)} %wg.1) | copy-start | bytes 1572868
  4.6 1.0 %copy-start.3 = (bf16[256,1024]{1,0:T(8,128)(2,1)S(1)}, bf16[256,1024]{1,0:T(8,128)(2,1)}, u32[]{:S(2)}) copy-start(bf16[256,1024]{1,0:T(8,128)(2,1)} %wdown.1) | copy-start | bytes 1572868
  5.7 0.7 %copy-start.4 = (s32[2048]{0:T(1024)S(1)}, s32[2048]{0:T(1024)}, u32[]{:S(2)}) copy-start(s32[2048]{0:T(1024)} %param.10) | copy-start | bytes 24580
  6.4 0.7 %copy-start.5 = (s32[2048]{0:T(1024)S(1)}, s32[2048]{0:T(1024)}, u32[]{:S(2)}) copy-start(s32[2048]{0:T(1024)} %param.11) | copy-start | bytes 24580
  7.1 0.7 %copy-start.6 = (bf16[9,256]{1,0:T(8,128)(2,1)S(1)}, bf16[9,256]{1,0:T(8,128)(2,1)}, u32[]{:S(2)}) copy-start(bf16[9,256]{1,0:T(8,128)(2,1)} %taps.1) | copy-start | bytes 13828

commit v2 on v1

--- a/solution.py
+++ b/solution.py
@@ -22,8 +22,9 @@
 
 def kernel(
     n_tm,
-    feat, starts, ends, wv, wg, taps, gain, shift, wdown,
+    feat, starts_in, ends_in, wv_in, wg_in, taps_in, gain_in, shift_in, wdown,
     out,
+    wv, wg, starts, ends, taps, gain, shift,
     xg, wo, wd, par, back, fwd, glu, conv, stat, norm, sw, ob,
     loc, wy_s, wy_r, wf_s, wf_r, par_s, par_r, fc_s, fc_r, fy_s, fy_r, ff_s, ff_r,
     ha_s, ha_r, wd_s, wd_r, st_s, st_r, sw_s, sw_r, oy_s, oy_r,
@@ -58,6 +59,27 @@
     def landed(ref, sem):
         pltpu.make_async_copy(ref, ref, sem).wait()
 
+    keep = pltpu.make_async_copy(
+        feat.at[pl.ds(pl.multiple_of(y * rows, rows), rows)], xg.at[chan], loc.at[0]
+    )
+    loads = [
+        pltpu.make_async_copy(src, dst, loc.at[3 + i])
+        for i, (src, dst) in enumerate(
+            (
+                (starts_in, starts),
+                (ends_in, ends),
+                (taps_in, taps),
+                (gain_in, gain),
+                (shift_in, shift),
+                (wv_in, wv),
+                (wg_in, wg),
+            )
+        )
+    ]
+    for copy in loads:
+        copy.start()
+    keep.start()
+
     barrier = pltpu.get_barrier_semaphore()
 
     def greet(i, c):
@@ -77,7 +99,7 @@
     mine = pl.ds(pl.multiple_of(g * piece, piece), piece)
     cross = [
         send(w.at[mine], wo.at[k, mine], wy_s.at[k], wy_r.at[k], across)
-        for k, w in enumerate((wv, wg))
+        for k, w in enumerate((wv_in, wg_in))
     ]
     for copy in cross:
         copy.start()
@@ -110,19 +132,19 @@
             xg.at[slot, part_rows(i)], xg.at[slot, part_rows(i)], ff_s.at[i], ff_r.at[i], beside
         )
 
-    keep = pltpu.make_async_copy(
-        feat.at[pl.ds(pl.multiple_of(y * rows, rows), rows)], xg.at[chan], loc.at[0]
-    )
-    keep.start()
     for i in range(PARTS):
         feat_beside(order(i)).start()
 
+    for copy in loads[:5]:
+        copy.wait()
+    gain_row = gain[...].astype(F32).reshape(1, width)
+    shift_row = shift[...].astype(F32).reshape(1, width)
     for q in range(2):
         lanes = slice(q * LANES, (q + 1) * LANES)
         par[2 * y + q] = jnp.zeros(par.shape[1:], F32)
         par[2 * y + q, 0:n_tap, :] = taps[:, lanes].astype(F32)
-        par[2 * y + q, n_tap : n_tap + 1, :] = gain[:, lanes].astype(F32)
-        par[2 * y + q, n_tap + 1 : n_tap + 2, :] = shift[:, lanes].astype(F32)
+        par[2 * y + q, n_tap : n_tap + 1, :] = gain_row[:, lanes]
+        par[2 * y + q, n_tap + 1 : n_tap + 2, :] = shift_row[:, lanes]
     my_par = par.at[pl.ds(2 * y, 2)]
     par_copy = send(my_par, my_par, par_s, par_r, across)
     par_copy.start()
@@ -157,6 +179,8 @@
     for i in range(1, PARTS):
         feat_across(order(i)).start()
     keep.wait()
+    for copy in loads[5:]:
+        copy.wait()
 
     def gated(i, half, value_w, gate_w):
         x = jnp.concatenate([xg[j, part_rows(i), :] for j in range(4)], axis=1)
@@ -352,9 +376,16 @@
     return pl.pallas_call(
         functools.partial(kernel, n_tm),
         out_shape=jax.ShapeDtypeStruct((frames, width), BF16),
-        in_specs=[vmem] * 9,
+        in_specs=[pl.BlockSpec(memory_space=pltpu.HBM)] * 9,
         out_specs=vmem,
         scratch_shapes=[
+            pltpu.VMEM((depth, width), BF16),
+            pltpu.VMEM((depth, width), BF16),
+            pltpu.VMEM((frames // LANES, LANES), jnp.int32),
+            pltpu.VMEM((frames // LANES, LANES), jnp.int32),
+            pltpu.VMEM(depth_kernel.shape, BF16),
+            pltpu.VMEM((width,), BF16),
+            pltpu.VMEM((width,), BF16),
             pltpu.VMEM((4, rows, width), BF16),
             pltpu.VMEM((2, depth, width), BF16),
             pltpu.VMEM((2, 4 * width, width), BF16),
@@ -367,7 +398,7 @@
             pltpu.VMEM((8, LANES), F32),
             pltpu.VMEM((2, 2, rows, width), BF16),
             pltpu.VMEM((rows, width), BF16),
-            dma((3,)),
+            dma((10,)),
             dma((2,)), dma((2,)),
             dma((2, GROUP)), dma((2, GROUP)),
             dma, dma,
@@ -381,7 +412,7 @@
             dma((STEPS,)), dma((STEPS,)),
         ],
         compiler_params=pltpu.CompilerParams(
-            collective_id=0, has_side_effects=True, vmem_limit_bytes=40 * 1024 * 1024
+            collective_id=0, has_side_effects=True, vmem_limit_bytes=62 * 1024 * 1024
         ),
     )(
         features,
@@ -390,8 +421,8 @@
         w_value,
         w_gate,
         depth_kernel,
-        norm_gain.reshape(1, -1),
-        norm_shift.reshape(1, -1),
+        norm_gain,
+        norm_shift,
         w_down,
     )
 

time: 67.3 us -> 61.7 us (0.917)
  local copies, waits for them, and re-layouts: 8.72 us -> 2.26 us
  Pallas kernels: 58.1 us -> 59.3 us
    unnamed x19 -> x1, local copies, waits for them, and re-layouts: 8.71 us -> 2.26 us
    pallas_call x1, Pallas kernels: 58.1 us -> 59.3 us  [body(): pl.pallas_call(functools.partial(kernel, n_tm), out_shape=jax.ShapeDtypeS...]
where the time goes in v2:
time: 61.7 us; the launch traced here: 61.6 us
  Pallas kernels  59.3 us (96%)
  local copies, waits for them, and re-layouts  2.26 us (4%)
    pallas_call x1, Pallas kernels, body(): pl.pallas_call(functools.partial(kernel, n_tm), out_shape=jax.ShapeDtypeS...  59.3 us
    unnamed x1, local copies, waits for them, and re-layouts  2.26 us

profile of v2, /device:TPU:0, one launch (start us, length us, event | category | flops | bytes accessed | tf_op | source)
XLA Modules:
  0.0 61.6 jit_solution(2809691750400333371)
XLA Ops:
  0.0 59.3 %shard_map.91 = bf16[2048,256]{1,0:T(8,128)(2,1)} custom-call(bf16[2048,256]{1,0:T(8,128)(2,1)} %feat.1, s32[16,128]{1,0:T(8,128)} %bitcast.2, s32[16,128]{1,0:T(8,128)} %bitcast.3, bf16[1024,256]{1,0:T(8,128)(2,1)} %wv_in.1, bf16[1024,256]{1,0:T(8,128)(2,1)} %wg_in.1, bf16[9,256]{1,0:T(8,128)(2,1)} %taps_in.1, bf16[256]{0:T(256)(128)(2,1)} %gain_in.1, ...), custom_call_target="tpu_custom_call" | custom-call | tf_op jit(solution)/shard_map/pallas_call | solution.py:376
  59.3 2.3 %copy.11 = bf16[2048,256]{1,0:T(8,128)(2,1)} copy(bf16[2048,256]{1,0:T(8,128)(2,1)} %shard_map.91) | data formatting | bytes 2097152

commit v3 on v2

--- a/solution.py
+++ b/solution.py
@@ -25,9 +25,9 @@
     feat, starts_in, ends_in, wv_in, wg_in, taps_in, gain_in, shift_in, wdown,
     out,
     wv, wg, starts, ends, taps, gain, shift,
-    xg, wo, wd, par, back, fwd, glu, conv, stat, norm, sw, ob,
+    xg, wo, wd, wdx, par, back, fwd, glu, conv, stat, norm, sw, ob,
     loc, wy_s, wy_r, wf_s, wf_r, par_s, par_r, fc_s, fc_r, fy_s, fy_r, ff_s, ff_r,
-    ha_s, ha_r, wd_s, wd_r, st_s, st_r, sw_s, sw_r, oy_s, oy_r,
+    ha_s, ha_r, wx_s, wx_r, wb_s, wb_r, wd_s, wd_r, st_s, st_r, sw_s, sw_r, oy_s, oy_r,
 ):
     depth, width = wv.shape
     rows = feat.shape[0] // 2
@@ -44,7 +44,6 @@
     me = 2 * t + y
     across = (t, 2 * oy + core)
     beside = (t, 2 * y + 1 - core)
-    diag = (t, 2 * oy + 1 - core)
     group, g = t - t % GROUP, t % GROUP
 
     def at_block(b):
@@ -90,11 +89,12 @@
         return c
 
     lax.fori_loop(1, n_blocks, greet, 0)
-    for other in (beside, diag):
+    for i in range(GROUP):
         pl.semaphore_signal(
-            barrier, inc=1, device_id=other, device_id_type=pl.DeviceIdType.MESH
-        )
-    pl.semaphore_wait(barrier, n_blocks + 1)
+            barrier, inc=1, device_id=(group + (g + i) % GROUP, beside[1]),
+            device_id_type=pl.DeviceIdType.MESH,
+        )
+    pl.semaphore_wait(barrier, n_blocks - 1 + GROUP)
 
     mine = pl.ds(pl.multiple_of(g * piece, piece), piece)
     cross = [
@@ -191,55 +191,63 @@
         glu[2 * half, to, :] = both[:, :LANES]
         glu[2 * half + 1, to, :] = both[:, LANES:]
 
-    def first_half(n, c):
-        i = order(n)
+    def first_half(i):
         feat_across(i).wait_recv()
         feat_forward(i).start()
         feat_beside(i).wait_recv()
         feat_forward(i).wait_recv()
         gated(i, y, wv[...], wg[...])
-        return c
-
-    lax.fori_loop(0, PARTS, first_half, 0)
-
-    def down_copy(p, h):
-        to = (beside, across, diag)[p]
-        to_core = to[1] % 2
-        cols = pl.ds(pl.multiple_of((2 * h + to_core) * width, width), width)
-        held = pl.ds(pl.multiple_of(chan * width, width), width)
+
+    def second_half(i):
+        gated(i, oy, wo[0], wo[1])
+
+    def halos(half):
+        pair = pl.ds(2 * half, 2)
+        return (
+            send(
+                glu.at[pair, pl.ds(rows, PAD)], glu.at[pair, pl.ds(0, PAD)],
+                ha_s.at[half, 0], ha_r.at[half, 0], at_block((me + 1) % n_blocks),
+            ),
+            send(
+                glu.at[pair, pl.ds(PAD, PAD)], glu.at[pair, pl.ds(rows + PAD, PAD)],
+                ha_s.at[half, 1], ha_r.at[half, 1], at_block((me + n_blocks - 1) % n_blocks),
+            ),
+        )
+
+    down_piece = width // GROUP
+    cut = pl.ds(pl.multiple_of(g * down_piece, down_piece), down_piece)
+    down_cross = send(wdown.at[cut], wdx, wx_s, wx_r, across)
+
+    def down_cols(h, c):
+        return pl.ds(pl.multiple_of((2 * h + c) * width, width), width)
+
+    own_held = pl.ds(pl.multiple_of(chan * width, width), width)
+
+    def down_beside(h):
         return send(
-            wdown.at[:, cols], wd.at[h, held], wd_s.at[p, h], wd_r.at[p, h], to
-        )
-
-    for h in range(2):
-        cols = pl.ds(pl.multiple_of((2 * h + core) * width, width), width)
-        held = pl.ds(pl.multiple_of(chan * width, width), width)
-        pltpu.make_async_copy(wdown.at[:, cols], wd.at[h, held], loc.at[1 + h]).start()
-
-    for k in range(2):
-        for i in range(1, GROUP):
-            share(k, i).wait_recv()
-
-    def second_half(n, c):
-        gated(order(n), oy, wo[0], wo[1])
-        return c
-
-    lax.fori_loop(0, 2, second_half, 0)
-    right = send(
-        glu.at[:, pl.ds(rows, PAD)], glu.at[:, pl.ds(0, PAD)], ha_s.at[0], ha_r.at[0],
-        at_block((me + 1) % n_blocks),
-    )
-    left = send(
-        glu.at[:, pl.ds(PAD, PAD)], glu.at[:, pl.ds(rows + PAD, PAD)], ha_s.at[1], ha_r.at[1],
-        at_block((me + n_blocks - 1) % n_blocks),
-    )
-    right.start()
-    left.start()
-    for p in range(3):
-        for h in range(2):
-            down_copy(p, h).start()
-    lax.fori_loop(2, PARTS, second_half, 0)
-    par_copy.wait_recv()
+            wdown.at[:, down_cols(h, 1 - core)], wd.at[h, own_held], wb_s.at[h], wb_r.at[h], beside
+        )
+
+    def down_keep(h):
+        return pltpu.make_async_copy(
+            wdown.at[:, down_cols(h, core)], wd.at[h, own_held], loc.at[1 + h]
+        )
+
+    def down_share(o, i, h):
+        to_core = (core, 1 - core)[o]
+        held = pl.ds(
+            pl.multiple_of(across[1] * width + g * down_piece, down_piece), down_piece
+        )
+        src, dst = wdx.at[:, down_cols(h, to_core)], wd.at[h, held]
+        if o == 0 and i == 0:
+            return pltpu.make_async_copy(src, dst, loc.at[10 + h])
+        to = (group + (g + i) % GROUP, 2 * y + to_core)
+        return send(src, dst, wd_s.at[o, i, h], wd_r.at[o, i, h], to)
+
+    shares = [
+        (o, i, h) for i in (1, 2, 3, 0) for o in range(2) for h in range(2) if (o, i) != (0, 0)
+    ]
+    kept = [(0, 0, h) for h in range(2)]
 
     def convolve(q, b):
         at = pl.multiple_of(b * BLOCK, BLOCK)
@@ -255,18 +263,51 @@
             acc = acc + term
         conv[q, pl.ds(at, BLOCK), :] = acc
 
+    last = order(PARTS - 1)
     n_inner = rows // BLOCK
-
-    def inner(b, c):
-        for q in range(4):
-            convolve(q, b)
-        return c
-
-    lax.fori_loop(1, n_inner - 1, inner, 0)
-    right.wait_recv()
-    left.wait_recv()
-    inner(0, 0)
-    inner(n_inner - 1, 0)
+    low, high = last * part // BLOCK - 1, (last + 1) * part // BLOCK + 1
+
+    def inner(half):
+        def run(b, c):
+            for q in range(2):
+                convolve(2 * half + q, b)
+            return c
+
+        return run
+
+    first, final = order(0), order(1)
+    first_half(first)
+    first_half(final)
+    for copy in halos(y):
+        copy.start()
+    for n in range(2, PARTS - 1):
+        first_half(order(n))
+    for k in range(2):
+        for i in range(1, GROUP):
+            share(k, i).wait_recv()
+    second_half(first)
+    second_half(final)
+    for copy in halos(oy):
+        copy.start()
+    down_cross.start()
+    for h in range(2):
+        down_keep(h).start()
+        down_beside(h).start()
+    for n in range(2, PARTS - 1):
+        second_half(order(n))
+    par_copy.wait_recv()
+    for half in (y, oy):
+        for copy in halos(half):
+            copy.wait_recv()
+        lax.fori_loop(0, low, inner(half), 0)
+        lax.fori_loop(high, n_inner, inner(half), 0)
+    down_cross.wait_recv()
+    for key in shares + kept:
+        down_share(*key).start()
+    first_half(last)
+    second_half(last)
+    for half in (y, oy):
+        lax.fori_loop(low, high, inner(half), 0)
 
     for q in range(4):
         block = conv[q]
@@ -319,12 +360,12 @@
 
     activate(0)
     for h in range(2):
-        held = pl.ds(pl.multiple_of(chan * width, width), width)
-        pltpu.make_async_copy(
-            wdown.at[:, pl.ds(0, width)], wd.at[h, held], loc.at[1 + h]
-        ).wait()
-        for p in range(3):
-            down_copy(p, h).wait_recv()
+        down_keep(h).wait()
+        down_beside(h).wait_recv()
+    for key in shares:
+        down_share(*key).wait_recv()
+    for key in kept:
+        down_share(*key).wait()
 
     def advance(c, carry):
         activate(c + 1)
@@ -337,14 +378,17 @@
     for copy in cross:
         copy.wait_send()
     par_copy.wait_send()
-    right.wait_send()
-    left.wait_send()
+    for half in (y, oy):
+        for copy in halos(half):
+            copy.wait_send()
     for k in range(2):
         for i in range(1, GROUP):
             share(k, i).wait_send()
-    for p in range(3):
-        for h in range(2):
-            down_copy(p, h).wait_send()
+    down_cross.wait_send()
+    for h in range(2):
+        down_beside(h).wait_send()
+    for key in shares:
+        down_share(*key).wait_send()
     landed(stat.at[pl.ds(0, n_blocks - 1)], st_s)
 
     def drain(i, c):
@@ -389,6 +433,7 @@
             pltpu.VMEM((4, rows, width), BF16),
             pltpu.VMEM((2, depth, width), BF16),
             pltpu.VMEM((2, 4 * width, width), BF16),
+            pltpu.VMEM((width // GROUP, 4 * width), BF16),
             pltpu.VMEM((4, 16, LANES), F32),
             pltpu.VMEM((rows, LANES), F32),
             pltpu.VMEM((rows, LANES), F32),
@@ -398,15 +443,17 @@
             pltpu.VMEM((8, LANES), F32),
             pltpu.VMEM((2, 2, rows, width), BF16),
             pltpu.VMEM((rows, width), BF16),
-            dma((10,)),
+            dma((12,)),
             dma((2,)), dma((2,)),
             dma((2, GROUP)), dma((2, GROUP)),
             dma, dma,
             dma((PARTS,)), dma((PARTS,)),
             dma((PARTS,)), dma((PARTS,)),
             dma((PARTS,)), dma((PARTS,)),
+            dma((2, 2)), dma((2, 2)),
+            dma, dma,
             dma((2,)), dma((2,)),
-            dma((3, 2)), dma((3, 2)),
+            dma((2, GROUP, 2)), dma((2, GROUP, 2)),
             dma, dma,
             dma((STEPS,)), dma((STEPS,)),
             dma((STEPS,)), dma((STEPS,)),

time: 61.7 us -> 59.7 us (0.968)
  Pallas kernels: 59.3 us -> 57.3 us
    pallas_call x1, Pallas kernels: 59.3 us -> 57.3 us  [body(): pl.pallas_call(functools.partial(kernel, n_tm), out_shape=jax.ShapeDtypeS...]
where the time goes in v3:
time: 59.7 us; the launch traced here: 59.5 us
  Pallas kernels  57.3 us (96%)
  local copies, waits for them, and re-layouts  2.26 us (4%)
    pallas_call x1, Pallas kernels, body(): pl.pallas_call(functools.partial(kernel, n_tm), out_shape=jax.ShapeDtypeS...  57.3 us
    unnamed x1, local copies, waits for them, and re-layouts  2.26 us

profile of v3, /device:TPU:0, one launch (start us, length us, event | category | flops | bytes accessed | tf_op | source)
XLA Modules:
  0.0 59.5 jit_solution(8766461553613226601)
XLA Ops:
  0.0 57.3 %shard_map.91 = bf16[2048,256]{1,0:T(8,128)(2,1)} custom-call(bf16[2048,256]{1,0:T(8,128)(2,1)} %feat.1, s32[16,128]{1,0:T(8,128)} %bitcast.2, s32[16,128]{1,0:T(8,128)} %bitcast.3, bf16[1024,256]{1,0:T(8,128)(2,1)} %wv_in.1, bf16[1024,256]{1,0:T(8,128)(2,1)} %wg_in.1, bf16[9,256]{1,0:T(8,128)(2,1)} %taps_in.1, bf16[256]{0:T(256)(128)(2,1)} %gain_in.1, ...), custom_call_target="tpu_custom_call" | custom-call | tf_op jit(solution)/shard_map/pallas_call | solution.py:420
  57.3 2.3 %copy.11 = bf16[2048,256]{1,0:T(8,128)(2,1)} copy(bf16[2048,256]{1,0:T(8,128)(2,1)} %shard_map.91) | data formatting | bytes 2097152

commit v4 on v3

--- a/solution.py
+++ b/solution.py
@@ -101,8 +101,7 @@
         send(w.at[mine], wo.at[k, mine], wy_s.at[k], wy_r.at[k], across)
         for k, w in enumerate((wv_in, wg_in))
     ]
-    for copy in cross:
-        copy.start()
+    cross[0].start()
 
     def own_rows(i):
         return pl.ds(pl.multiple_of(y * rows + i * part, part), part)
@@ -135,6 +134,8 @@
     for i in range(PARTS):
         feat_beside(order(i)).start()
 
+    cross[0].wait_send()
+    cross[1].start()
     for copy in loads[:5]:
         copy.wait()
     gain_row = gain[...].astype(F32).reshape(1, width)
@@ -164,23 +165,37 @@
         back[tile, :] = jnp.broadcast_to(before[r : r + 1, :], (LANES, LANES)).T
         fwd[tile, :] = jnp.broadcast_to(after[r : r + 1, :], (LANES, LANES)).T
 
+    near = (g + 1 - 2 * (g % 2), (g + 2) % GROUP)
+
     def share(k, i):
         return send(
             wo.at[k, mine], wo.at[k, mine], wf_s.at[k, i], wf_r.at[k, i],
-            (group + (g + i) % GROUP, chan),
+            (group + near[i], chan),
+        )
+
+    def relay(k, i):
+        held = pl.ds(pl.multiple_of(near[i] * piece + i * (piece // 2), piece // 2), piece // 2)
+        return send(
+            wo.at[k, held], wo.at[k, held], wf_s.at[k, 2 + i], wf_r.at[k, 2 + i],
+            (group + near[1 - i], chan),
         )
 
     for k in range(2):
         cross[k].wait_recv()
-        for i in range(1, GROUP):
+        for i in range(2):
             share(k, i).start()
         if k == 0:
+            cross[1].wait_send()
             feat_across(order(0)).start()
     for i in range(1, PARTS):
         feat_across(order(i)).start()
     keep.wait()
     for copy in loads[5:]:
         copy.wait()
+    for k in range(2):
+        for i in range(2):
+            share(k, i).wait_recv()
+            relay(k, i).start()
 
     def gated(i, half, value_w, gate_w):
         x = jnp.concatenate([xg[j, part_rows(i), :] for j in range(4)], axis=1)
@@ -280,20 +295,20 @@
     first_half(final)
     for copy in halos(y):
         copy.start()
-    for n in range(2, PARTS - 1):
-        first_half(order(n))
     for k in range(2):
-        for i in range(1, GROUP):
-            share(k, i).wait_recv()
+        for i in range(2):
+            relay(k, i).wait_recv()
     second_half(first)
     second_half(final)
     for copy in halos(oy):
         copy.start()
-    down_cross.start()
     for h in range(2):
         down_keep(h).start()
         down_beside(h).start()
     for n in range(2, PARTS - 1):
+        first_half(order(n))
+        if n == PARTS - 2:
+            down_cross.start()
         second_half(order(n))
     par_copy.wait_recv()
     for half in (y, oy):
@@ -375,15 +390,14 @@
     lax.fori_loop(0, STEPS - 1, advance, 0)
     project(STEPS - 1)
 
-    for copy in cross:
-        copy.wait_send()
     par_copy.wait_send()
     for half in (y, oy):
         for copy in halos(half):
             copy.wait_send()
     for k in range(2):
-        for i in range(1, GROUP):
+        for i in range(2):
             share(k, i).wait_send()
+            relay(k, i).wait_send()
     down_cross.wait_send()
     for h in range(2):
         down_beside(h).wait_send()

time: 59.7 us -> 59.2 us (level)
  Pallas kernels: 57.3 us -> 56.7 us
where the time goes in v4:
time: 59.2 us; the launch traced here: 59 us
  Pallas kernels  56.7 us (96%)
  local copies, waits for them, and re-layouts  2.26 us (4%)
    pallas_call x1, Pallas kernels, body(): pl.pallas_call(functools.partial(kernel, n_tm), out_shape=jax.ShapeDtypeS...  56.7 us
    unnamed x1, local copies, waits for them, and re-layouts  2.26 us

profile of v4, /device:TPU:0, one launch (start us, length us, event | category | flops | bytes accessed | tf_op | source)
XLA Modules:
  0.0 59.0 jit_solution(16732671172874989424)
XLA Ops:
  0.0 56.7 %shard_map.91 = bf16[2048,256]{1,0:T(8,128)(2,1)} custom-call(bf16[2048,256]{1,0:T(8,128)(2,1)} %feat.1, s32[16,128]{1,0:T(8,128)} %bitcast.2, s32[16,128]{1,0:T(8,128)} %bitcast.3, bf16[1024,256]{1,0:T(8,128)(2,1)} %wv_in.1, bf16[1024,256]{1,0:T(8,128)(2,1)} %wg_in.1, bf16[9,256]{1,0:T(8,128)(2,1)} %taps_in.1, bf16[256]{0:T(256)(128)(2,1)} %gain_in.1, ...), custom_call_target="tpu_custom_call" | custom-call | tf_op jit(solution)/shard_map/pallas_call | solution.py:434
  56.7 2.3 %copy.11 = bf16[2048,256]{1,0:T(8,128)(2,1)} copy(bf16[2048,256]{1,0:T(8,128)(2,1)} %shard_map.91) | data formatting | bytes 2097152

commit v5 on v4

--- a/solution.py
+++ b/solution.py
@@ -9,7 +9,7 @@
 
 F32, BF16 = jnp.float32, jnp.bfloat16
 GROUP = 4
-PARTS = 4
+PARTS = 8
 STEPS = 8
 PAD = 8
 BLOCK = 64
@@ -112,8 +112,8 @@
     def part_rows(i):
         return pl.ds(pl.multiple_of(i * part, part), part)
 
-    def order(i):
-        return (3 * i) % PARTS
+    def order(n):
+        return (0, PARTS - 1)[n] if n < 2 else n - 1
 
     def feat_beside(i):
         return send(
@@ -278,9 +278,7 @@
             acc = acc + term
         conv[q, pl.ds(at, BLOCK), :] = acc
 
-    last = order(PARTS - 1)
     n_inner = rows // BLOCK
-    low, high = last * part // BLOCK - 1, (last + 1) * part // BLOCK + 1
 
     def inner(half):
         def run(b, c):
@@ -290,39 +288,45 @@
 
         return run
 
-    first, final = order(0), order(1)
-    first_half(first)
-    first_half(final)
-    for copy in halos(y):
-        copy.start()
+    early = PARTS // 2
+    for n in range(early):
+        first_half(order(n))
+        if n == 1:
+            for copy in halos(y):
+                copy.start()
     for k in range(2):
         for i in range(2):
             relay(k, i).wait_recv()
-    second_half(first)
-    second_half(final)
+    second_half(order(0))
+    second_half(order(1))
     for copy in halos(oy):
         copy.start()
     for h in range(2):
         down_keep(h).start()
         down_beside(h).start()
-    for n in range(2, PARTS - 1):
-        first_half(order(n))
-        if n == PARTS - 2:
-            down_cross.start()
+    for n in range(2, early):
         second_half(order(n))
     par_copy.wait_recv()
     for half in (y, oy):
         for copy in halos(half):
             copy.wait_recv()
-        lax.fori_loop(0, low, inner(half), 0)
-        lax.fori_loop(high, n_inner, inner(half), 0)
-    down_cross.wait_recv()
-    for key in shares + kept:
-        down_share(*key).start()
-    first_half(last)
-    second_half(last)
-    for half in (y, oy):
-        lax.fori_loop(low, high, inner(half), 0)
+    top = (PARTS - 1) * part // BLOCK + 1
+    done = 0
+    for n in range(early, PARTS):
+        first_half(order(n))
+        if n == PARTS - 2:
+            down_cross.start()
+        if n == PARTS - 1:
+            down_cross.wait_recv()
+            for key in shares + kept:
+                down_share(*key).start()
+        second_half(order(n))
+        ready = top if n == PARTS - 1 else n * part // BLOCK - 1
+        for half in (y, oy):
+            lax.fori_loop(done, ready, inner(half), 0)
+            if n == early:
+                lax.fori_loop(top, n_inner, inner(half), 0)
+        done = ready
 
     for q in range(4):
         block = conv[q]
@@ -421,6 +425,20 @@
     lax.fori_loop(0, STEPS, finish, 0)
 
 
+def settle(src, dst, sem):
+    rows = src.shape[0] // STEPS
+    copies = [
+        pltpu.make_async_copy(
+            src.at[pl.ds(i * rows, rows)], dst.at[pl.ds(i * rows, rows)], sem.at[i]
+        )
+        for i in range(STEPS)
+    ]
+    for copy in copies:
+        copy.start()
+    for copy in copies:
+        copy.wait()
+
+
 def body(
     n_tm,
     features, rec_start, rec_end, w_value, w_gate, depth_kernel, norm_gain, norm_shift, w_down,
@@ -431,7 +449,7 @@
     dma = pltpu.SemaphoreType.DMA
     vmem = pl.BlockSpec(memory_space=pltpu.VMEM)
     n_blocks = 2 * n_tm
-    return pl.pallas_call(
+    mixed = pl.pallas_call(
         functools.partial(kernel, n_tm),
         out_shape=jax.ShapeDtypeStruct((frames, width), BF16),
         in_specs=[pl.BlockSpec(memory_space=pltpu.HBM)] * 9,
@@ -486,6 +504,15 @@
         norm_shift,
         w_down,
     )
+    hbm = pl.BlockSpec(memory_space=pltpu.HBM)
+    return pl.pallas_call(
+        settle,
+        out_shape=jax.ShapeDtypeStruct((frames, width), BF16),
+        in_specs=[hbm],
+        out_specs=hbm,
+        scratch_shapes=[dma((STEPS,))],
+        compiler_params=pltpu.CompilerParams(vmem_limit_bytes=62 * 1024 * 1024),
+    )(mixed)
 
 
 def solution(mesh):

time: 59.2 us -> 99 us (1.67)
  Pallas kernels: 56.7 us -> 98.9 us
  local copies, waits for them, and re-layouts: 2.26 us -> 0 us
    pallas_call x0 -> x1, Pallas kernels: none -> 32.9 us  [body(): pl.pallas_call(settle, out_shape=jax.ShapeDtypeStruct((frames, width), BF...]
    pallas_call x1, Pallas kernels: 56.7 us -> 66 us  [body(): pl.pallas_call(functools.partial(kernel, n_tm), out_shape=jax.ShapeDtypeS...]
    unnamed x1 -> x0, local copies, waits for them, and re-layouts: 2.26 us -> none
where the time goes in v5:
time: 99 us; the launch traced here: 98.9 us
  Pallas kernels  98.9 us (100%)
    pallas_call x1, Pallas kernels, body(): pl.pallas_call(functools.partial(kernel, n_tm), out_shape=jax.ShapeDtypeS...  66 us
    pallas_call x1, Pallas kernels, body(): pl.pallas_call(settle, out_shape=jax.ShapeDtypeStruct((frames, width), BF...  32.9 us

profile of v5, /device:TPU:0, one launch (start us, length us, event | category | flops | bytes accessed | tf_op | source)
XLA Modules:
  0.0 98.9 jit_solution(8493939234041869384)
XLA Ops:
  0.0 66.0 %shard_map.91.src = bf16[2048,256]{1,0:T(8,128)(2,1)} custom-call(bf16[2048,256]{1,0:T(8,128)(2,1)} %feat.1, s32[16,128]{1,0:T(8,128)} %bitcast.2, s32[16,128]{1,0:T(8,128)} %bitcast.3, bf16[1024,256]{1,0:T(8,128)(2,1)} %wv_in.1, bf16[1024,256]{1,0:T(8,128)(2,1)} %wg_in.1, bf16[9,256]{1,0:T(8,128)(2,1)} %taps_in.1, bf16[256]{0:T(256)(128)(2,1)} %gain_in.1, ...), custom_call_target="tpu_custom_call" | custom-call | tf_op jit(solution)/shard_map/pallas_call | solution.py:452
  66.0 32.9 %shard_map.92 = bf16[2048,256]{1,0:T(8,128)(2,1)} custom-call(bf16[2048,256]{1,0:T(8,128)(2,1)} %shard_map.91.src), custom_call_target="tpu_custom_call" | custom-call | tf_op jit(solution)/shard_map/pallas_call | solution.py:508

commit v6 on v4

--- a/solution.py
+++ b/solution.py
@@ -10,7 +10,8 @@
 F32, BF16 = jnp.float32, jnp.bfloat16
 GROUP = 4
 PARTS = 4
-STEPS = 8
+UNITS = 2
+STEPS = 4
 PAD = 8
 BLOCK = 64
 LANES = 128
@@ -24,12 +25,12 @@
     n_tm,
     feat, starts_in, ends_in, wv_in, wg_in, taps_in, gain_in, shift_in, wdown,
     out,
-    wv, wg, starts, ends, taps, gain, shift,
-    xg, wo, wd, wdx, par, back, fwd, glu, conv, stat, norm, sw, ob,
+    w, starts, ends, taps, gain, shift,
+    xg, wd, wdx, par, gap, back, fwd, glu, conv, stat, norm, sw, ob,
     loc, wy_s, wy_r, wf_s, wf_r, par_s, par_r, fc_s, fc_r, fy_s, fy_r, ff_s, ff_r,
     ha_s, ha_r, wx_s, wx_r, wb_s, wb_r, wd_s, wd_r, st_s, st_r, sw_s, sw_r, oy_s, oy_r,
 ):
-    depth, width = wv.shape
+    depth, width = wv_in.shape
     rows = feat.shape[0] // 2
     part, step_rows = rows // PARTS, rows // STEPS
     piece = depth // GROUP
@@ -70,8 +71,8 @@
                 (taps_in, taps),
                 (gain_in, gain),
                 (shift_in, shift),
-                (wv_in, wv),
-                (wg_in, wg),
+                (wv_in, w.at[y, 0]),
+                (wg_in, w.at[y, 1]),
             )
         )
     ]
@@ -98,8 +99,8 @@
 
     mine = pl.ds(pl.multiple_of(g * piece, piece), piece)
     cross = [
-        send(w.at[mine], wo.at[k, mine], wy_s.at[k], wy_r.at[k], across)
-        for k, w in enumerate((wv_in, wg_in))
+        send(mat.at[mine], w.at[y, k, mine], wy_s.at[k], wy_r.at[k], across)
+        for k, mat in enumerate((wv_in, wg_in))
     ]
     cross[0].start()
 
@@ -111,9 +112,6 @@
 
     def part_rows(i):
         return pl.ds(pl.multiple_of(i * part, part), part)
-
-    def order(i):
-        return (3 * i) % PARTS
 
     def feat_beside(i):
         return send(
@@ -132,7 +130,7 @@
         )
 
     for i in range(PARTS):
-        feat_beside(order(i)).start()
+        feat_beside(i).start()
 
     cross[0].wait_send()
     cross[1].start()
@@ -160,23 +158,28 @@
     )
     before = jnp.minimum(frame - starts[span, :], reach).astype(F32)
     after = jnp.minimum(ends[span, :] - 1 - frame, reach).astype(F32)
-    for r in range(groups):
-        tile = slice(r * LANES, (r + 1) * LANES)
-        back[tile, :] = jnp.broadcast_to(before[r : r + 1, :], (LANES, LANES)).T
-        fwd[tile, :] = jnp.broadcast_to(after[r : r + 1, :], (LANES, LANES)).T
+    gap[0], gap[1] = before, after
+
+    def spread(r, c):
+        tile = pl.ds(pl.multiple_of(r * LANES, LANES), LANES)
+        back[tile, :] = jnp.broadcast_to(gap[0, pl.ds(r, 1), :], (LANES, LANES)).T
+        fwd[tile, :] = jnp.broadcast_to(gap[1, pl.ds(r, 1), :], (LANES, LANES)).T
+        return c
+
+    lax.fori_loop(0, groups, spread, 0)
 
     near = (g + 1 - 2 * (g % 2), (g + 2) % GROUP)
 
     def share(k, i):
         return send(
-            wo.at[k, mine], wo.at[k, mine], wf_s.at[k, i], wf_r.at[k, i],
+            w.at[oy, k, mine], w.at[oy, k, mine], wf_s.at[k, i], wf_r.at[k, i],
             (group + near[i], chan),
         )
 
     def relay(k, i):
         held = pl.ds(pl.multiple_of(near[i] * piece + i * (piece // 2), piece // 2), piece // 2)
         return send(
-            wo.at[k, held], wo.at[k, held], wf_s.at[k, 2 + i], wf_r.at[k, 2 + i],
+            w.at[oy, k, held], w.at[oy, k, held], wf_s.at[k, 2 + i], wf_r.at[k, 2 + i],
             (group + near[1 - i], chan),
         )
 
@@ -186,9 +189,9 @@
             share(k, i).start()
         if k == 0:
             cross[1].wait_send()
-            feat_across(order(0)).start()
+            feat_across(0).start()
     for i in range(1, PARTS):
-        feat_across(order(i)).start()
+        feat_across(i).start()
     keep.wait()
     for copy in loads[5:]:
         copy.wait()
@@ -197,24 +200,23 @@
             share(k, i).wait_recv()
             relay(k, i).start()
 
-    def gated(i, half, value_w, gate_w):
-        x = jnp.concatenate([xg[j, part_rows(i), :] for j in range(4)], axis=1)
-        value = jnp.dot(x, value_w, preferred_element_type=F32)
-        gate = jnp.dot(x, gate_w, preferred_element_type=F32)
+    unit = rows // UNITS
+    per_unit = PARTS // UNITS
+
+    def gated(i, half):
+        at = pl.ds(pl.multiple_of(i * unit, unit), unit)
+        x = jnp.concatenate([xg[j, at, :] for j in range(4)], axis=1)
+        value = jnp.dot(x, w[half, 0], preferred_element_type=F32)
+        gate = jnp.dot(x, w[half, 1], preferred_element_type=F32)
         both = swish_gate(value, gate).astype(BF16).astype(F32)
-        to = pl.ds(pl.multiple_of(PAD + i * part, PAD), part)
+        to = pl.ds(pl.multiple_of(PAD + i * unit, PAD), unit)
         glu[2 * half, to, :] = both[:, :LANES]
         glu[2 * half + 1, to, :] = both[:, LANES:]
 
-    def first_half(i):
+    def arrive(i):
         feat_across(i).wait_recv()
         feat_forward(i).start()
         feat_beside(i).wait_recv()
-        feat_forward(i).wait_recv()
-        gated(i, y, wv[...], wg[...])
-
-    def second_half(i):
-        gated(i, oy, wo[0], wo[1])
 
     def halos(half):
         pair = pl.ds(2 * half, 2)
@@ -278,58 +280,74 @@
             acc = acc + term
         conv[q, pl.ds(at, BLOCK), :] = acc
 
-    last = order(PARTS - 1)
     n_inner = rows // BLOCK
-    low, high = last * part // BLOCK - 1, (last + 1) * part // BLOCK + 1
-
-    def inner(half):
-        def run(b, c):
-            for q in range(2):
-                convolve(2 * half + q, b)
+    per_block = unit // BLOCK
+
+    def inner(b, c):
+        def one(q, c):
+            convolve(q, b)
             return c
 
-        return run
-
-    first, final = order(0), order(1)
-    first_half(first)
-    first_half(final)
-    for copy in halos(y):
-        copy.start()
-    for k in range(2):
-        for i in range(2):
-            relay(k, i).wait_recv()
-    second_half(first)
-    second_half(final)
-    for copy in halos(oy):
-        copy.start()
-    for h in range(2):
-        down_keep(h).start()
-        down_beside(h).start()
-    for n in range(2, PARTS - 1):
-        first_half(order(n))
-        if n == PARTS - 2:
+        return lax.fori_loop(0, 4, one, c)
+
+    def settle(i, c):
+        lax.fori_loop(i * per_unit, (i + 1) * per_unit, lambda n, c: arrive(n) or c, 0)
+
+        @pl.when(i == UNITS - 1)
+        def _():
             down_cross.start()
-        second_half(order(n))
-    par_copy.wait_recv()
+
+        lax.fori_loop(
+            i * per_unit, (i + 1) * per_unit, lambda n, c: feat_forward(n).wait_recv() or c, 0
+        )
+
+        def product(j, c):
+            @pl.when((i == 0) & (j == 1))
+            def _():
+                for k in range(2):
+                    for n in range(2):
+                        relay(k, n).wait_recv()
+
+            gated(i, (y + j) % 2)
+            return c
+
+        lax.fori_loop(0, 2, product, 0)
+
+        @pl.when(i == 0)
+        def _():
+            par_copy.wait_recv()
+            for h in range(2):
+                down_keep(h).start()
+                down_beside(h).start()
+
+        @pl.when(i == UNITS - 1)
+        def _():
+            for half in (y, oy):
+                for copy in halos(half):
+                    copy.start()
+
+        low = jnp.where(i == 0, 1, i * per_block - 1)
+        lax.fori_loop(low, (i + 1) * per_block - 1, inner, 0)
+        return c
+
+    lax.fori_loop(0, UNITS, settle, 0)
+    down_cross.wait_recv()
+    for key in shares + kept:
+        down_share(*key).start()
     for half in (y, oy):
         for copy in halos(half):
             copy.wait_recv()
-        lax.fori_loop(0, low, inner(half), 0)
-        lax.fori_loop(high, n_inner, inner(half), 0)
-    down_cross.wait_recv()
-    for key in shares + kept:
-        down_share(*key).start()
-    first_half(last)
-    second_half(last)
-    for half in (y, oy):
-        lax.fori_loop(low, high, inner(half), 0)
-
-    for q in range(4):
+    lax.fori_loop(0, 2, lambda n, c: inner(n * (n_inner - 1), c), 0)
+
+    def gather(q, c):
         block = conv[q]
         total_q = jnp.sum(block, axis=0, keepdims=True)
         off = block - total_q * (1.0 / rows)
-        stat[me, q : q + 1, :] = total_q
-        stat[me, 4 + q : 5 + q, :] = jnp.sum(off * off, axis=0, keepdims=True)
+        stat[me, pl.ds(q, 1), :] = total_q
+        stat[me, pl.ds(4 + q, 1), :] = jnp.sum(off * off, axis=0, keepdims=True)
+        return c
+
+    lax.fori_loop(0, 4, gather, 0)
 
     def tell(i, c):
         send(stat.at[me], stat.at[me], st_s, st_r, at_block((me + i) % n_blocks)).start()
@@ -373,22 +391,22 @@
         give(c).start()
         out[home_rows(c), :] = jnp.dot(x, wd[y], preferred_element_type=F32).astype(BF16)
 
-    activate(0)
-    for h in range(2):
-        down_keep(h).wait()
-        down_beside(h).wait_recv()
-    for key in shares:
-        down_share(*key).wait_recv()
-    for key in kept:
-        down_share(*key).wait()
+    def ready():
+        for h in range(2):
+            down_keep(h).wait()
+            down_beside(h).wait_recv()
+        for key in shares:
+            down_share(*key).wait_recv()
+        for key in kept:
+            down_share(*key).wait()
 
     def advance(c, carry):
-        activate(c + 1)
-        project(c)
+        pl.when(c < STEPS)(lambda: activate(c))
+        pl.when(c == 1)(ready)
+        pl.when(c > 0)(lambda: project(c - 1))
         return carry
 
-    lax.fori_loop(0, STEPS - 1, advance, 0)
-    project(STEPS - 1)
+    lax.fori_loop(0, STEPS + 1, advance, 0)
 
     par_copy.wait_send()
     for half in (y, oy):
@@ -437,18 +455,17 @@
         in_specs=[pl.BlockSpec(memory_space=pltpu.HBM)] * 9,
         out_specs=vmem,
         scratch_shapes=[
-            pltpu.VMEM((depth, width), BF16),
-            pltpu.VMEM((depth, width), BF16),
+            pltpu.VMEM((2, 2, depth, width), BF16),
             pltpu.VMEM((frames // LANES, LANES), jnp.int32),
             pltpu.VMEM((frames // LANES, LANES), jnp.int32),
             pltpu.VMEM(depth_kernel.shape, BF16),
             pltpu.VMEM((width,), BF16),
             pltpu.VMEM((width,), BF16),
             pltpu.VMEM((4, rows, width), BF16),
-            pltpu.VMEM((2, depth, width), BF16),
             pltpu.VMEM((2, 4 * width, width), BF16),
             pltpu.VMEM((width // GROUP, 4 * width), BF16),
             pltpu.VMEM((4, 16, LANES), F32),
+            pltpu.VMEM((2, rows // LANES, LANES), F32),
             pltpu.VMEM((rows, LANES), F32),
             pltpu.VMEM((rows, LANES), F32),
             pltpu.VMEM((4, rows + 2 * PAD, LANES), F32),

time: 59.2 us -> 58.9 us (level)
  no operation moved by 1% of the time
where the time goes in v6:
time: 58.9 us; the launch traced here: 58.8 us
  Pallas kernels  56.5 us (96%)
  local copies, waits for them, and re-layouts  2.26 us (4%)
    pallas_call x1, Pallas kernels, body(): pl.pallas_call(functools.partial(kernel, n_tm), out_shape=jax.ShapeDtypeS...  56.5 us
    unnamed x1, local copies, waits for them, and re-layouts  2.26 us

profile of v6, /device:TPU:0, one launch (start us, length us, event | category | flops | bytes accessed | tf_op | source)
XLA Modules:
  0.0 58.8 jit_solution(8491725176875108607)
XLA Ops:
  0.0 56.5 %shard_map.91 = bf16[2048,256]{1,0:T(8,128)(2,1)} custom-call(bf16[2048,256]{1,0:T(8,128)(2,1)} %feat.1, s32[16,128]{1,0:T(8,128)} %bitcast.2, s32[16,128]{1,0:T(8,128)} %bitcast.3, bf16[1024,256]{1,0:T(8,128)(2,1)} %wv_in.1, bf16[1024,256]{1,0:T(8,128)(2,1)} %wg_in.1, bf16[9,256]{1,0:T(8,128)(2,1)} %taps_in.1, bf16[256]{0:T(256)(128)(2,1)} %gain_in.1, ...), custom_call_target="tpu_custom_call" | custom-call | tf_op jit(solution)/shard_map/pallas_call | solution.py:452
  56.5 2.3 %copy.11 = bf16[2048,256]{1,0:T(8,128)(2,1)} copy(bf16[2048,256]{1,0:T(8,128)(2,1)} %shard_map.91) | data formatting | bytes 2097152

commit v7 on v6

--- a/solution.py
+++ b/solution.py
@@ -10,10 +10,10 @@
 F32, BF16 = jnp.float32, jnp.bfloat16
 GROUP = 4
 PARTS = 4
-UNITS = 2
+UNITS = 4
 STEPS = 4
 PAD = 8
-BLOCK = 64
+BLOCK = 32
 LANES = 128
 
 
@@ -266,71 +266,66 @@
     ]
     kept = [(0, 0, h) for h in range(2)]
 
-    def convolve(q, b):
+    def inner(b, c):
         at = pl.multiple_of(b * BLOCK, BLOCK)
         room_back, room_fwd = back[pl.ds(at, BLOCK), :], fwd[pl.ds(at, BLOCK), :]
-        acc = jnp.zeros((BLOCK, LANES), F32)
+        accs = [jnp.zeros((BLOCK, LANES), F32)] * 4
         for k in range(n_tap):
             d = k - reach
-            term = glu[q, pl.ds(at + (PAD + d), BLOCK), :] * par[q, k : k + 1, :]
-            if d < 0:
-                term = jnp.where(room_back >= float(-d), term, 0.0)
-            elif d > 0:
-                term = jnp.where(room_fwd >= float(d), term, 0.0)
-            acc = acc + term
-        conv[q, pl.ds(at, BLOCK), :] = acc
+            usable = room_back >= float(-d) if d < 0 else room_fwd >= float(d)
+            for q in range(4):
+                term = glu[q, pl.ds(at + (PAD + d), BLOCK), :] * par[q, k : k + 1, :]
+                accs[q] = accs[q] + (term if d == 0 else jnp.where(usable, term, 0.0))
+        for q in range(4):
+            conv[q, pl.ds(at, BLOCK), :] = accs[q]
+        return c
 
     n_inner = rows // BLOCK
     per_block = unit // BLOCK
 
-    def inner(b, c):
-        def one(q, c):
-            convolve(q, b)
-            return c
-
-        return lax.fori_loop(0, 4, one, c)
-
     def settle(i, c):
-        lax.fori_loop(i * per_unit, (i + 1) * per_unit, lambda n, c: arrive(n) or c, 0)
+        @pl.when(i < UNITS)
+        def _():
+            lax.fori_loop(i * per_unit, (i + 1) * per_unit, lambda n, c: arrive(n) or c, 0)
 
         @pl.when(i == UNITS - 1)
         def _():
             down_cross.start()
 
-        lax.fori_loop(
-            i * per_unit, (i + 1) * per_unit, lambda n, c: feat_forward(n).wait_recv() or c, 0
-        )
-
-        def product(j, c):
-            @pl.when((i == 0) & (j == 1))
-            def _():
-                for k in range(2):
-                    for n in range(2):
-                        relay(k, n).wait_recv()
-
-            gated(i, (y + j) % 2)
-            return c
-
-        lax.fori_loop(0, 2, product, 0)
-
-        @pl.when(i == 0)
+        @pl.when(i == 1)
         def _():
+            for k in range(2):
+                for n in range(2):
+                    relay(k, n).wait_recv()
             par_copy.wait_recv()
             for h in range(2):
                 down_keep(h).start()
                 down_beside(h).start()
 
-        @pl.when(i == UNITS - 1)
+        @pl.when(i > 0)
         def _():
-            for half in (y, oy):
-                for copy in halos(half):
-                    copy.start()
-
-        low = jnp.where(i == 0, 1, i * per_block - 1)
-        lax.fori_loop(low, (i + 1) * per_block - 1, inner, 0)
-        return c
-
-    lax.fori_loop(0, UNITS, settle, 0)
+            u = i - 1
+            gated(u, oy)
+
+            @pl.when(u == UNITS - 1)
+            def _():
+                for half in (y, oy):
+                    for copy in halos(half):
+                        copy.start()
+
+            low = jnp.where(u == 0, 1, u * per_block - 1)
+            lax.fori_loop(low, (u + 1) * per_block - 1, inner, 0)
+
+        @pl.when(i < UNITS)
+        def _():
+            lax.fori_loop(
+                i * per_unit, (i + 1) * per_unit, lambda n, c: feat_forward(n).wait_recv() or c, 0
+            )
+            gated(i, y)
+
+        return c
+
+    lax.fori_loop(0, UNITS + 1, settle, 0)
     down_cross.wait_recv()
     for key in shares + kept:
         down_share(*key).start()

time: 58.9 us -> 59.4 us (level)
  no operation moved by 1% of the time
where the time goes in v7:
time: 59.4 us; the launch traced here: 59.3 us
  Pallas kernels  57 us (96%)
  local copies, waits for them, and re-layouts  2.26 us (4%)
    pallas_call x1, Pallas kernels, body(): pl.pallas_call(functools.partial(kernel, n_tm), out_shape=jax.ShapeDtypeS...  57 us
    unnamed x1, local copies, waits for them, and re-layouts  2.26 us

profile of v7, /device:TPU:0, one launch (start us, length us, event | category | flops | bytes accessed | tf_op | source)
XLA Modules:
  0.0 59.3 jit_solution(3234142266241918365)
XLA Ops:
  0.0 57.0 %shard_map.91 = bf16[2048,256]{1,0:T(8,128)(2,1)} custom-call(bf16[2048,256]{1,0:T(8,128)(2,1)} %feat.1, s32[16,128]{1,0:T(8,128)} %bitcast.2, s32[16,128]{1,0:T(8,128)} %bitcast.3, bf16[1024,256]{1,0:T(8,128)(2,1)} %wv_in.1, bf16[1024,256]{1,0:T(8,128)(2,1)} %wg_in.1, bf16[9,256]{1,0:T(8,128)(2,1)} %taps_in.1, bf16[256]{0:T(256)(128)(2,1)} %gain_in.1, ...), custom_call_target="tpu_custom_call" | custom-call | tf_op jit(solution)/shard_map/pallas_call | solution.py:447
  57.0 2.3 %copy.11 = bf16[2048,256]{1,0:T(8,128)(2,1)} copy(bf16[2048,256]{1,0:T(8,128)(2,1)} %shard_map.91) | data formatting | bytes 2097152

commit v8 on v7

--- a/solution.py
+++ b/solution.py
@@ -11,7 +11,7 @@
 GROUP = 4
 PARTS = 4
 UNITS = 4
-STEPS = 4
+STEPS = 8
 PAD = 8
 BLOCK = 32
 LANES = 128
@@ -288,7 +288,7 @@
         def _():
             lax.fori_loop(i * per_unit, (i + 1) * per_unit, lambda n, c: arrive(n) or c, 0)
 
-        @pl.when(i == UNITS - 1)
+        @pl.when(i == UNITS - 2)
         def _():
             down_cross.start()
 
@@ -323,12 +323,15 @@
             )
             gated(i, y)
 
+        @pl.when(i == UNITS - 1)
+        def _():
+            down_cross.wait_recv()
+            for key in shares + kept:
+                down_share(*key).start()
+
         return c
 
     lax.fori_loop(0, UNITS + 1, settle, 0)
-    down_cross.wait_recv()
-    for key in shares + kept:
-        down_share(*key).start()
     for half in (y, oy):
         for copy in halos(half):
             copy.wait_recv()

time: 59.4 us -> 62.1 us (1.045)
  Pallas kernels: 57 us -> 59.7 us
    pallas_call x1, Pallas kernels: 57 us -> 59.7 us  [body(): pl.pallas_call(functools.partial(kernel, n_tm), out_shape=jax.ShapeDtypeS...]
where the time goes in v8:
time: 62.1 us; the launch traced here: 61.9 us
  Pallas kernels  59.7 us (96%)
  local copies, waits for them, and re-layouts  2.26 us (4%)
    pallas_call x1, Pallas kernels, body(): pl.pallas_call(functools.partial(kernel, n_tm), out_shape=jax.ShapeDtypeS...  59.7 us
    unnamed x1, local copies, waits for them, and re-layouts  2.26 us

profile of v8, /device:TPU:0, one launch (start us, length us, event | category | flops | bytes accessed | tf_op | source)
XLA Modules:
  0.0 61.9 jit_solution(17449753481850178714)
XLA Ops:
  0.0 59.7 %shard_map.91 = bf16[2048,256]{1,0:T(8,128)(2,1)} custom-call(bf16[2048,256]{1,0:T(8,128)(2,1)} %feat.1, s32[16,128]{1,0:T(8,128)} %bitcast.2, s32[16,128]{1,0:T(8,128)} %bitcast.3, bf16[1024,256]{1,0:T(8,128)(2,1)} %wv_in.1, bf16[1024,256]{1,0:T(8,128)(2,1)} %wg_in.1, bf16[9,256]{1,0:T(8,128)(2,1)} %taps_in.1, bf16[256]{0:T(256)(128)(2,1)} %gain_in.1, ...), custom_call_target="tpu_custom_call" | custom-call | tf_op jit(solution)/shard_map/pallas_call | solution.py:450
  59.7 2.3 %copy.11 = bf16[2048,256]{1,0:T(8,128)(2,1)} copy(bf16[2048,256]{1,0:T(8,128)(2,1)} %shard_map.91) | data formatting | bytes 2097152

commit v9 on v6

--- a/solution.py
+++ b/solution.py
@@ -384,12 +384,18 @@
     def give(c):
         return send(ob.at[step_at(c)], out.at[home_rows(c)], oy_s.at[c], oy_r.at[c], across)
 
+    def mixed(c, half):
+        x = jnp.concatenate([sw[j % 2, j // 2, step_at(c), :] for j in range(4)], axis=1)
+        return jnp.dot(x, wd[half], preferred_element_type=F32).astype(BF16)
+
     def project(c):
         pass_on(c).wait_recv()
-        x = jnp.concatenate([sw[j % 2, j // 2, step_at(c), :] for j in range(4)], axis=1)
-        ob[step_at(c), :] = jnp.dot(x, wd[oy], preferred_element_type=F32).astype(BF16)
+        ob[step_at(c), :] = mixed(c, oy)
         give(c).start()
-        out[home_rows(c), :] = jnp.dot(x, wd[y], preferred_element_type=F32).astype(BF16)
+
+    def stay(c, carry):
+        out[home_rows(c), :] = mixed(c, y)
+        return carry
 
     def ready():
         for h in range(2):
@@ -407,6 +413,7 @@
         return carry
 
     lax.fori_loop(0, STEPS + 1, advance, 0)
+    lax.fori_loop(0, STEPS, stay, 0)
 
     par_copy.wait_send()
     for half in (y, oy):

time: 58.9 us -> 58.8 us (level)
  no operation moved by 1% of the time
where the time goes in v9:
time: 58.8 us; the launch traced here: 58.7 us
  Pallas kernels  56.4 us (96%)
  local copies, waits for them, and re-layouts  2.26 us (4%)
    pallas_call x1, Pallas kernels, body(): pl.pallas_call(functools.partial(kernel, n_tm), out_shape=jax.ShapeDtypeS...  56.4 us
    unnamed x1, local copies, waits for them, and re-layouts  2.26 us

profile of v9, /device:TPU:0, one launch (start us, length us, event | category | flops | bytes accessed | tf_op | source)
XLA Modules:
  0.0 58.7 jit_solution(853555561033171419)
XLA Ops:
  0.0 56.4 %shard_map.91 = bf16[2048,256]{1,0:T(8,128)(2,1)} custom-call(bf16[2048,256]{1,0:T(8,128)(2,1)} %feat.1, s32[16,128]{1,0:T(8,128)} %bitcast.2, s32[16,128]{1,0:T(8,128)} %bitcast.3, bf16[1024,256]{1,0:T(8,128)(2,1)} %wv_in.1, bf16[1024,256]{1,0:T(8,128)(2,1)} %wg_in.1, bf16[9,256]{1,0:T(8,128)(2,1)} %taps_in.1, bf16[256]{0:T(256)(128)(2,1)} %gain_in.1, ...), custom_call_target="tpu_custom_call" | custom-call | tf_op jit(solution)/shard_map/pallas_call | solution.py:459
  56.4 2.3 %copy.11 = bf16[2048,256]{1,0:T(8,128)(2,1)} copy(bf16[2048,256]{1,0:T(8,128)(2,1)} %shard_map.91) | data formatting | bytes 2097152
